TPU v7x, 32 devices: a whole 2x2x4 slice. The times are simulated.
32 devices in a mesh: wave: 16 (over z, y, x), lev: 2 (over core).
Axes of the slice: x: 2, y: 2, z: 4, core: 2. Of those that a mesh axis runs over, the one named last changes fastest.
Arguments:
- fourier_in: bfloat16 [3, 28, 1280, 64], P(None, 'lev', 'wave'), may hold values from -6 to 6
- spectral_old: bfloat16 [3, 28, 16, 2816], P(None, 'lev', 'wave'), may hold values from -6 to 6
- legendre: bfloat16 [16, 1408, 1280], P('wave'), may hold values from -0.15625 to 0.15625
- g_matrix: float32 [28, 28], replicated, may hold values from -1 to 1
- modes_in: float32 [28, 28], replicated, may hold values from -1 to 1
- modes_out: float32 [28, 28], replicated, may hold values from -1 to 1
- mode_heating: float32 [28, 28], replicated, may hold values from -1 to 1
- mode_rates: float32 [28], replicated, may hold values from 0.1 to 10
- pair_ids: int32 [16], replicated, may hold values from 0 to 639, as said below
- lat_ids: int32 [1280], replicated, may hold values from 0 to 1279, each once
- limits: int32 [1280], replicated, may hold values from 10 to 1280
Outputs:
- spectral_new: bfloat16 [3, 28, 16, 2816], P(None, 'lev', 'wave')
- fourier_out: bfloat16 [3, 28, 1280, 64], P(None, 'lev', 'wave')
Inputs may be any that keep to these rules, and one draw needn't show every extreme that they name: `pair_ids`: distinct pair numbers. `lat_ids`: each latitude once.
All inputs are finite; a program needn't handle non-finite values.
Results may differ from a plain program's by a relative error of at most 0.018.
Values may be sent and summed in bfloat16 or wider, within the bound.
A program may use at most 64 MiB of HBM per device.

v0:
```python
import jax
import jax.numpy as jnp
from jax import lax
from jax.sharding import PartitionSpec as P

MMAX = 1280
BLOCK = 64
coupling = 2.0
highest = lax.Precision.HIGHEST


def pair_layout(pair_number, row_count):
    row_index = jnp.arange(row_count, dtype=jnp.int32)
    first_length = MMAX - pair_number
    first_pad = (first_length + BLOCK - 1) // BLOCK * BLOCK
    in_first = row_index < first_pad
    row_valid = jnp.where(
        in_first, row_index < first_length, row_index - first_pad < pair_number + 1
    )
    degree = jnp.where(
        in_first, pair_number + row_index, MMAX - 1 - pair_number + row_index - first_pad
    ).astype(jnp.float32)
    lfactor = degree * (degree + 1.0) / float(MMAX * (MMAX - 1))
    return (row_valid, lfactor, first_pad)


def level_term(matrix, vector, level_start, lev_count, row_start, row_total):
    rows_block = lax.dynamic_slice(
        matrix, (jnp.asarray(row_start, jnp.int32), level_start), (row_total, lev_count)
    )
    return jnp.dot(rows_block, vector, precision=highest, preferred_element_type=jnp.float32)


def legendre_forward(stacked, pair_table, first_pad, pair_number, row_count):
    column_count = stacked.shape[1]

    def block_step(block_index, running, which_wave):
        start_row = block_index * BLOCK
        table_rows = lax.dynamic_slice_in_dim(pair_table, start_row, BLOCK, 0)
        product = lax.dot_general(
            stacked[which_wave],
            table_rows,
            (((1,), (1,)), ((), ())),
            preferred_element_type=jnp.float32,
        )
        return lax.dynamic_update_slice_in_dim(running, product, start_row, 1)

    running = jnp.zeros((column_count, row_count), jnp.float32)
    split_block = first_pad // BLOCK
    end_block = (first_pad + pair_number + BLOCK) // BLOCK
    running = lax.fori_loop(
        0, split_block, lambda block_index, carried: block_step(block_index, carried, 0), running
    )
    running = lax.fori_loop(
        split_block,
        end_block,
        lambda block_index, carried: block_step(block_index, carried, 1),
        running,
    )
    return running


def legendre_inverse(slot_spectra, pair_table, first_pad, pair_number):
    column_count = slot_spectra.shape[0]
    lat_total = pair_table.shape[1]

    def block_step(block_index, running):
        start_row = block_index * BLOCK
        table_rows = lax.dynamic_slice_in_dim(pair_table, start_row, BLOCK, 0)
        spectra_rows = lax.dynamic_slice_in_dim(slot_spectra, start_row, BLOCK, 1)
        return running + jnp.dot(spectra_rows, table_rows, preferred_element_type=jnp.float32)

    zeros_grid = jnp.zeros((column_count, lat_total), jnp.float32)
    split_block = first_pad // BLOCK
    end_block = (first_pad + pair_number + BLOCK) // BLOCK
    first_wave = lax.fori_loop(0, split_block, block_step, zeros_grid)
    second_wave = lax.fori_loop(split_block, end_block, block_step, zeros_grid)
    return jnp.stack([first_wave, second_wave])


def body(
    fourier_in,
    spectral_old,
    legendre,
    g_matrix,
    modes_in,
    modes_out,
    mode_heating,
    mode_rates,
    pair_ids,
    lat_ids,
    limits,
):
    lev_count = fourier_in.shape[1]
    lat_count = fourier_in.shape[2]
    pair_count = legendre.shape[0]
    row_count = legendre.shape[1]
    lat_total = legendre.shape[2]
    wave_index = lax.axis_index("wave")
    level_start = lax.axis_index("lev") * lev_count
    pair_slot = 0
    pair_number = lax.dynamic_slice_in_dim(pair_ids, wave_index * pair_count + pair_slot, 1)[0]
    layouts = [(pair_number,) + pair_layout(pair_number, row_count)]
    own_lats = lax.dynamic_slice_in_dim(lat_ids, wave_index * lat_count, lat_count)
    matches = own_lats[:, None] == jnp.arange(lat_total, dtype=jnp.int32)[None, :]
    row_limit = jnp.sum(jnp.where(matches, limits[None, :], 0), axis=1)
    both_waves = jnp.stack([pair_ids, MMAX - 1 - pair_ids], axis=1)
    column_wave = jnp.repeat(both_waves, 2, axis=1).reshape(-1)
    keep_mask = column_wave[None, :] < row_limit[:, None]
    masked = jnp.where(keep_mask[None, None], fourier_in, jnp.zeros((), fourier_in.dtype))
    exchanged = lax.all_to_all(masked, "wave", split_axis=3, concat_axis=2, tiled=True)
    item_count = exchanged.shape[0]
    column_count = item_count * lev_count * 2
    pair_slot = 0
    pair_number, row_valid, lfactor, first_pad = layouts[pair_slot]
    slot_data = exchanged.reshape(item_count, lev_count, lat_total, 2, 2)
    stacked = jnp.transpose(slot_data, (3, 0, 1, 4, 2)).reshape(2, column_count, lat_total)
    spectra = legendre_forward(stacked, legendre[pair_slot], first_pad, pair_number, row_count)
    spectra = jnp.where(row_valid[None, :], spectra, 0.0)
    results = [spectra.reshape(item_count, lev_count, 2, row_count)]
    tendency = jnp.stack(results, axis=2)
    flat_size = pair_count * 2 * row_count
    old_fields = spectral_old.reshape(3, lev_count, pair_count, 2, row_count).astype(jnp.float32)
    vorticity = (old_fields[0] + tendency[0]).reshape(lev_count, flat_size)
    divergence = (old_fields[1] + tendency[1]).reshape(lev_count, flat_size)
    heat_star = (old_fields[2] + tendency[2]).reshape(lev_count, flat_size)
    wave_factor = jnp.stack(
        [jnp.broadcast_to(layout[2][None, :], (2, row_count)) for layout in layouts]
    ).reshape(1, flat_size)
    keep_rows = jnp.stack(
        [jnp.broadcast_to(layout[1][None, :], (2, row_count)) for layout in layouts]
    ).reshape(1, flat_size)
    rates_own = lax.dynamic_slice_in_dim(mode_rates, level_start, lev_count)
    hydrostatic = lax.psum_scatter(
        level_term(
            g_matrix,
            heat_star,
            level_start,
            lev_count,
            jnp.int32(0),
            lev_count * lax.axis_size("lev"),
        ).astype(jnp.bfloat16),
        "lev",
        scatter_dimension=0,
        tiled=True,
    ).astype(jnp.float32)
    right_own = divergence + coupling * wave_factor * hydrostatic
    projected = lax.psum_scatter(
        level_term(
            modes_in,
            right_own,
            level_start,
            lev_count,
            jnp.int32(0),
            lev_count * lax.axis_size("lev"),
        ).astype(jnp.bfloat16),
        "lev",
        scatter_dimension=0,
        tiled=True,
    ).astype(jnp.float32)
    modal_part = projected / (1.0 + coupling * coupling * wave_factor * rates_own[:, None])
    row_start = jnp.int32(0)
    row_total = lev_count * lax.axis_size("lev")
    divergence_part = level_term(
        modes_out, modal_part, level_start, lev_count, row_start, row_total
    )
    heating_part = level_term(
        mode_heating, modal_part, level_start, lev_count, row_start, row_total
    )
    rebuilt = lax.psum_scatter(
        jnp.stack([divergence_part, heating_part], axis=1).astype(jnp.bfloat16),
        "lev",
        scatter_dimension=0,
        tiled=True,
    ).astype(jnp.float32)
    vorticity_out = jnp.where(keep_rows, vorticity, 0.0).astype(jnp.bfloat16)
    divergence_out = jnp.where(keep_rows, rebuilt[:, 0], 0.0).astype(jnp.bfloat16)
    heat_out = jnp.where(keep_rows, heat_star - coupling * rebuilt[:, 1], 0.0).astype(jnp.bfloat16)
    spectral_new = jnp.stack([vorticity_out, divergence_out, heat_out]).reshape(
        3, lev_count, pair_count, 2 * row_count
    )
    pair_slot = 0
    pair_number, row_valid, lfactor, first_pad = layouts[pair_slot]
    slot_spectra = spectral_new[:, :, pair_slot].reshape(3 * lev_count * 2, row_count)
    grid_part = legendre_inverse(slot_spectra, legendre[pair_slot], first_pad, pair_number)
    grid_part = (
        grid_part.reshape(2, 3, lev_count, 2, lat_total)
        .transpose(1, 2, 4, 0, 3)
        .reshape(3, lev_count, lat_total, 4)
    )
    gridded = grid_part.astype(jnp.bfloat16)
    returned = lax.all_to_all(gridded, "wave", split_axis=2, concat_axis=3, tiled=True)
    fourier_out = jnp.where(keep_mask[None, None], returned, jnp.zeros((), jnp.bfloat16))
    return (spectral_new, fourier_out)


def solution(mesh):
    placed = (
        P(None, "lev", "wave", None),
        P(None, "lev", "wave", None),
        P("wave", None, None),
        P(),
        P(),
        P(),
        P(),
        P(),
        P(),
        P(),
        P(),
    )
    return jax.shard_map(
        body,
        mesh=mesh,
        in_specs=placed,
        out_specs=(P(None, "lev", "wave", None), P(None, "lev", "wave", None)),
        check_vma=False,
    )
```

profile of v0, /device:TPU:0, one launch (start us, length us, event | category | flops | bytes accessed | tf_op | source)
XLA Modules:
  0.0 189.5 jit_solution(12464096708221175484)
XLA Ops:
  11.8 1.3 copy.81
  13.1 8.3 %all-to-all-start = ((bf16[3,14,80,64]{2,1,0,3:T(8,128)(2,1)}), bf16[3,14,80,64]{2,1,0,3:T(8,128)(2,1)S(1)}, u32[]{:S(2)}, u32[]{:S(2)}) async-start(bf16[3,14,80,64]{2,1,0,3:T(8,128)(2,1)} %copy.81), calls=%async_computation | async-start | bytes 1572864 | tf_op jit(solution)/shard_map/all_to_all | solution.py:111
  25.5 15.7 %all-to-all-done = bf16[3,14,80,64]{2,1,0,3:T(8,128)(2,1)S(1)} async-done(((bf16[3,14,80,64]{2,1,0,3:T(8,128)(2,1)}), bf16[3,14,80,64]{2,1,0,3:T(8,128)(2,1)S(1)}, u32[]{:S(2)}, u32[]{:S(2)}) %all-to-all-start) | async-done | bytes 430112 | tf_op jit(solution)/shard_map/all_to_all | solution.py:111
  43.2 19.2 %while.40 = (s32[]{:T(128)}, f32[84,1408]{0,1:T(8,128)S(1)}, s32[]{:T(128)}, bf16[1408,1280]{1,0:T(8,128)(2,1)}, bf16[2,84,1280]{2,1,0:T(8,128)(2,1)S(1)}, /*index=5*/s32[]{:T(128)}, s32[]{:T(128)}, s32[]{:T(128)}, s32[]{:T(128)}) while((s32[]{:T(128)}, f32[84,1408]{0,1:T(8,128)S(1)}, s32[]{:T(128)}, bf16[1408,1280]{1,0:T(8,128)(2,1)}, ...), condition=%wide.region_2.3_spmd, body=%wide.region_1.2_spmd.sunk | while | flops 13762566 | bytes 423051 | solution.py:51
  62.4 4.5 %while.41 = (s32[]{:T(128)}, f32[84,1408]{0,1:T(8,128)S(1)}, s32[]{:T(128)}, bf16[1408,1280]{1,0:T(8,128)(2,1)}, bf16[2,84,1280]{2,1,0:T(8,128)(2,1)S(1)}, /*index=5*/s32[]{:T(128)}, s32[]{:T(128)}, s32[]{:T(128)}, s32[]{:T(128)}) while((s32[]{:T(128)}, f32[84,1408]{0,1:T(8,128)S(1)}, s32[]{:T(128)}, bf16[1408,1280]{1,0:T(8,128)(2,1)}, ...), condition=%wide.region_4.5_spmd, body=%wide.region_3.4_spmd.sunk | while | flops 13762566 | bytes 423051 | solution.py:54
  68.6 3.0 %fusion = bf16[16,2816]{1,0:T(8,128)(2,1)S(1)} fusion(bf16[28,2816]{1,0:T(8,128)(2,1)S(1)} %convolution_convert_fusion.3), kind=kCustom, calls=%all-reduce-scatter | all-reduce-scatter fusion | flops 90113 | bytes 248320
  71.6 2.3 %collective-permute-start = (bf16[2,2816]{1,0:T(2,128)(2,1)S(1)}, bf16[2,2816]{1,0:T(2,128)(2,1)S(1)}, u32[]{:S(2)}, u32[]{:S(2)}) collective-permute-start(bf16[2,2816]{1,0:T(2,128)(2,1)S(1)} %slice.52), channel_id=1, source_target_pairs={{0,1},{2,3},{4,5},{6,7},{8,9},{10,11},{12,13},{14,15},{16,17},{18,... | collective-permute-start | bytes 33800
  76.9 3.0 %fusion.1 = bf16[16,2816]{1,0:T(8,128)(2,1)S(1)} fusion(bf16[28,2816]{1,0:T(8,128)(2,1)S(1)} %convolution_convert_fusion.2), kind=kCustom, calls=%all-reduce-scatter.1 | all-reduce-scatter fusion | flops 90113 | bytes 248320
  80.0 2.3 %collective-permute-start.1 = (bf16[2,2816]{1,0:T(2,128)(2,1)S(1)}, bf16[2,2816]{1,0:T(2,128)(2,1)S(1)}, u32[]{:S(2)}, u32[]{:S(2)}) collective-permute-start(bf16[2,2816]{1,0:T(2,128)(2,1)S(1)} %slice.53), channel_id=1, source_target_pairs={{0,1},{2,3},{4,5},{6,7},{8,9},{10,11},{12,13},{14,15},{16,17},{18,... | collective-permute-start | bytes 33800
  86.6 16.7 %all-reduce.7.cloned.1.call-done = bf16[28,2,2816]{2,1,0:T(2,128)(2,1)} async-done(((bf16[28,2,2816]{2,1,0:T(2,128)(2,1)}), bf16[28,2,2816]{2,1,0:T(2,128)(2,1)}) %all-reduce.7.cloned.1.call-update) | async-done | bytes 315408
  105.4 4.9 %while.43 = (s32[]{:T(128)}, f32[84,1280]{1,0:T(8,128)S(1)}, s32[]{:T(128)}, bf16[84,1408]{1,0:T(8,128)(2,1)S(1)}, bf16[1408,1280]{1,0:T(8,128)(2,1)}, /*index=5*/s32[]{:T(128)}, s32[]{:T(128)}, s32[]{:T(128)}, s32[]{:T(128)}) while((s32[]{:T(128)}, f32[84,1280]{1,0:T(8,128)S(1)}, s32[]{:T(128)}, bf16[84,1408]{1,0:T(8,128)(2,1)S(1)}, ...), condition=%wide.region_11.12_spmd, body=%wide.region_10.11_spmd.sunk | while | flops 13870086 | bytes 1068171 | solution.py:77
  106.6 1.2 convolution_add_fusion.5
  109.1 1.2 convolution_add_fusion.5
  110.4 20.7 %while.42 = (s32[]{:T(128)}, f32[84,1280]{1,0:T(8,128)S(1)}, s32[]{:T(128)}, bf16[84,1408]{1,0:T(8,128)(2,1)S(1)}, bf16[1408,1280]{1,0:T(8,128)(2,1)}, /*index=5*/s32[]{:T(128)}, s32[]{:T(128)}, s32[]{:T(128)}, s32[]{:T(128)}) while((s32[]{:T(128)}, f32[84,1280]{1,0:T(8,128)S(1)}, s32[]{:T(128)}, bf16[84,1408]{1,0:T(8,128)(2,1)S(1)}, ...), condition=%wide.region_9.10_spmd, body=%wide.region_8.9_spmd.sunk | while | flops 13870086 | bytes 1068171 | solution.py:76
  110.5 1.2 convolution_add_fusion.4
  111.7 1.2 convolution_add_fusion.4
  112.9 1.2 convolution_add_fusion.4
  114.1 1.2 convolution_add_fusion.4
  115.3 1.2 convolution_add_fusion.4
  117.8 1.2 convolution_add_fusion.4
  120.2 1.2 convolution_add_fusion.4
  121.4 1.2 convolution_add_fusion.4
  122.6 1.2 convolution_add_fusion.4
  123.9 1.2 convolution_add_fusion.4
  125.1 1.2 convolution_add_fusion.4
  127.5 1.2 convolution_add_fusion.4
  129.9 1.2 convolution_add_fusion.4
  131.9 6.4 %copy.98 = bf16[3,14,1280,2,2]{1,4,3,0,2:T(2,128)(2,1)} copy(bf16[3,14,1280,2,2]{2,4,3,1,0:T(2,128)(2,1)S(1)} %maximum_bitcast_fusion) | data formatting | bytes 860160 | tf_op jit(solution)/shard_map/convert_element_type | solution.py:191
  138.3 6.7 %reshape.298 = bf16[16,2,6720]{2,1,0:T(2,128)(2,1)S(1)} reshape(bf16[1280,3,4,14]{3,2,1,0:T(4,128)(2,1)} %bitcast.96) | data formatting | bytes 860160
  145.0 20.5 %all_to_all.33 = bf16[16,2,6720]{2,1,0:T(2,128)(2,1)S(1)} all-to-all(bf16[16,2,6720]{2,1,0:T(2,128)(2,1)S(1)} %reshape.298), channel_id=1, replica_groups=mesh['wave'=16,'lev'=2] {'wave'}, dimensions={0} | all-to-all | bytes 860160 | tf_op jit(solution)/shard_map/all_to_all | solution.py:192
  165.5 10.5 %reshape.299 = bf16[1280,3,4,14]{3,2,1,0:T(4,128)(2,1)} reshape(bf16[16,2,6720]{2,1,0:T(2,128)(2,1)S(1)} %all_to_all.33) | data formatting | bytes 860160
  175.9 5.5 %copy.99 = bf16[3,14,16,80,4]{3,2,4,1,0:T(8,128)(2,1)S(1)} copy(bf16[3,14,16,80,4]{1,4,0,3,2:T(4,128)(2,1)} %bitcast.97) | data formatting | bytes 860160 | tf_op jit(solution)/shard_map/all_to_all | solution.py:192
  (107 shorter events, 49.2 us)
Async XLA Ops:
  7.2 60.9 %copy-start = (f32[28,28]{1,0:T(8,128)S(1)}, f32[28,28]{1,0:T(8,128)}, u32[]{:S(2)}) copy-start(f32[28,28]{1,0:T(8,128)} %param.22) | copy-start | bytes 9412
  7.2 14.3 %copy-start.4 = (s32[16]{0:T(128)S(1)}, s32[16]{0:T(128)}, u32[]{:S(2)}) copy-start(s32[16]{0:T(128)} %param.27) | copy-start | bytes 196
  7.2 18.2 %copy-start.1 = (bf16[3,14,1,2816]{3,1,2,0:T(8,128)(2,1)S(1)}, bf16[3,14,1,2816]{3,1,2,0:T(8,128)(2,1)}, u32[]{:S(2)}) copy-start(bf16[3,14,1,2816]{3,1,2,0:T(8,128)(2,1)} %param.20) | copy-start | bytes 709636
  13.1 28.1 %all-to-all-start = ((bf16[3,14,80,64]{2,1,0,3:T(8,128)(2,1)}), bf16[3,14,80,64]{2,1,0,3:T(8,128)(2,1)S(1)}, u32[]{:S(2)}, u32[]{:S(2)}) async-start(bf16[3,14,80,64]{2,1,0,3:T(8,128)(2,1)} %copy.81), calls=%async_computation | async-start | bytes 1572864 | tf_op jit(solution)/shard_map/all_to_all | solution.py:111
  21.5 81.9 %all-reduce.7.cloned.1.call-start = ((), (), s32[]{:S(2)}) async-start(), calls=%async_computation.2 | async-start | bytes 630784
  67.0 7.6 %copy-start.3 = (u32[32]{0:T(128)S(1)}, u32[32]{0:T(128)}, u32[]{:S(2)}) copy-start(u32[32]{0:T(128)} %constant.117) | copy-start | bytes 388
  67.2 9.2 %copy-start.2 = (f32[28,28]{1,0:T(8,128)S(1)}, f32[28,28]{1,0:T(8,128)}, u32[]{:S(2)}) copy-start(f32[28,28]{1,0:T(8,128)} %param.23) | copy-start | bytes 9412
  67.3 15.0 %copy-start.7 = (f32[28]{0:T(128)S(1)}, f32[28]{0:T(128)}, u32[]{:S(2)}) copy-start(f32[28]{0:T(128)} %param.26) | copy-start | bytes 340
  67.3 16.1 %copy-start.5 = (f32[28,28]{1,0:T(8,128)S(1)}, f32[28,28]{1,0:T(8,128)}, u32[]{:S(2)}) copy-start(f32[28,28]{1,0:T(8,128)} %param.25) | copy-start | bytes 9412
  67.7 16.1 %copy-start.6 = (f32[28,28]{1,0:T(8,128)S(1)}, f32[28,28]{1,0:T(8,128)}, u32[]{:S(2)}) copy-start(f32[28,28]{1,0:T(8,128)} %param.24) | copy-start | bytes 9412
  71.6 4.5 %collective-permute-start = (bf16[2,2816]{1,0:T(2,128)(2,1)S(1)}, bf16[2,2816]{1,0:T(2,128)(2,1)S(1)}, u32[]{:S(2)}, u32[]{:S(2)}) collective-permute-start(bf16[2,2816]{1,0:T(2,128)(2,1)S(1)} %slice.52), channel_id=1, source_target_pairs={{0,1},{2,3},{4,5},{6,7},{8,9},{10,11},{12,13},{14,15},{16,17},{18,... | collective-permute-start | bytes 33800
  80.0 3.1 %collective-permute-start.1 = (bf16[2,2816]{1,0:T(2,128)(2,1)S(1)}, bf16[2,2816]{1,0:T(2,128)(2,1)S(1)}, u32[]{:S(2)}, u32[]{:S(2)}) collective-permute-start(bf16[2,2816]{1,0:T(2,128)(2,1)S(1)} %slice.53), channel_id=1, source_target_pairs={{0,1},{2,3},{4,5},{6,7},{8,9},{10,11},{12,13},{14,15},{16,17},{18,... | collective-permute-start | bytes 33800
Sparse Core Ops, SparseCore 0:
  85.6 17.6 all-reduce.6
where the time goes:
time: 191 us; the launch traced here: 190 us
  matrix products  50.2 us (26%)
  local copies, waits for them, and re-layouts  39.6 us (21%)
  waiting for transfers between devices  33.2 us (17%)
  blocking collectives  26.5 us (14%)
  between operations  19.2 us (10%)
  starting transfers between devices  12.9 us (7%)
  other arithmetic  6.88 us (4%)
    dot_general x21, matrix products, block_step(): jnp.dot(spectra_rows, table_rows, preferred_element_type=jnp.float32)  25 us
    dot_general x21, matrix products, block_step(): lax.dot_general(stacked[which_wave], table_rows, (((1,), (1,)), ((), ()))...  23.2 us
    all_to_all x1, blocking collectives, body(): lax.all_to_all(gridded, 'wave', split_axis=2, concat_axis=3, tiled=True)  20.5 us
    unnamed x24, local copies, waits for them, and re-layouts  19.4 us
    unnamed x4, waiting for transfers between devices  17.5 us
    all_to_all x1, waiting for transfers between devices, body(): lax.all_to_all(masked, 'wave', split_axis=3, concat_axis=2, tiled=True)  15.7 us
    all_to_all x1, starting transfers between devices, body(): lax.all_to_all(masked, 'wave', split_axis=3, concat_axis=2, tiled=True)  8.3 us
    convert_element_type x1, local copies, waits for them, and re-layouts, body(): gridded = grid_part.astype(jnp.bfloat16)  6.42 us
  transfers between devices with their start and end apart: 4, of which 3 were waited for; matrix products, arithmetic and copies ran while one was open for 1% of the time, Pallas kernels for 0%

commit v1 on v0

--- a/solution.py
+++ b/solution.py
@@ -7,6 +7,28 @@
 BLOCK = 64
 coupling = 2.0
 highest = lax.Precision.HIGHEST
+
+
+def split_up(x, dim, size):
+    before, after = (x.shape[:dim], x.shape[dim + 1 :])
+    return jnp.moveaxis(x.reshape(*before, size, -1, *after), dim, 0)
+
+
+def joined_along(parts, dim):
+    shape = list(parts.shape[1:])
+    shape[dim] *= parts.shape[0]
+    return jnp.moveaxis(parts, 0, dim).reshape(shape)
+
+
+def exchange_in_pairs(x, axis, split_dim, concat_dim):
+    devices, index = (lax.axis_size(axis), lax.axis_index(axis))
+    tiles = split_up(x, split_dim, devices)
+    outs = [tiles[index]]
+    for hop in range(1, devices):
+        sent = tiles[index ^ hop]
+        outs.append(lax.ppermute(sent, axis, [(i, i ^ hop) for i in range(devices)]))
+    tiles = jnp.stack(outs)[index ^ jnp.arange(devices)]
+    return joined_along(tiles, concat_dim)
 
 
 def pair_layout(pair_number, row_count):
@@ -189,7 +211,7 @@
         .reshape(3, lev_count, lat_total, 4)
     )
     gridded = grid_part.astype(jnp.bfloat16)
-    returned = lax.all_to_all(gridded, "wave", split_axis=2, concat_axis=3, tiled=True)
+    returned = exchange_in_pairs(gridded, "wave", 2, 3)
     fourier_out = jnp.where(keep_mask[None, None], returned, jnp.zeros((), jnp.bfloat16))
     return (spectral_new, fourier_out)
 

time: 191 us -> 181 us (0.948)
  starting transfers between devices: 12.9 us -> 40.3 us
  local copies, waits for them, and re-layouts: 39.6 us -> 14.9 us
  blocking collectives: 26.5 us -> 5.99 us
  waiting for transfers between devices: 33.2 us -> 40.3 us
    ppermute x0 -> x15, starting transfers between devices: none -> 27.4 us  [exchange_in_pairs(): lax.ppermute(sent, axis, [(i, i ^ hop) for i in range(devices)])]
    all_to_all x1 -> x0, blocking collectives: 20.5 us -> none  [body(): lax.all_to_all(gridded, 'wave', split_axis=2, concat_axis=3, tiled=True)]
    unnamed x24 -> x52, local copies, waits for them, and re-layouts: 19.4 us -> 2.9 us
    ppermute x0 -> x15, waiting for transfers between devices: none -> 7.3 us  [exchange_in_pairs(): lax.ppermute(sent, axis, [(i, i ^ hop) for i in range(devices)])]
    all_to_all x2 -> x0, local copies, waits for them, and re-layouts: 5.79 us -> none  [body(): lax.all_to_all(gridded, 'wave', split_axis=2, concat_axis=3, tiled=True)]
    convert_element_type x1, local copies, waits for them, and re-layouts: 6.42 us -> 0.82 us  [body(): gridded = grid_part.astype(jnp.bfloat16)]
  transfers between devices with their start and end apart: 4 -> 19, of which waited for: 3 -> 6; matrix products, arithmetic and copies ran while one was open for 1% -> 2% of each run, Pallas kernels for 0% -> 0%
where the time goes in v1:
time: 181 us; the launch traced here: 179 us
  matrix products  50.2 us (28%)
  starting transfers between devices  40.3 us (22%)
  waiting for transfers between devices  40.3 us (22%)
  between operations  19.5 us (11%)
  local copies, waits for them, and re-layouts  14.9 us (8%)
  other arithmetic  6.9 us (4%)
  blocking collectives  5.99 us (3%)
    ppermute x15, starting transfers between devices, exchange_in_pairs(): lax.ppermute(sent, axis, [(i, i ^ hop) for i in range(devices)])  27.4 us
    dot_general x21, matrix products, block_step(): jnp.dot(spectra_rows, table_rows, preferred_element_type=jnp.float32)  25 us
    dot_general x21, matrix products, block_step(): lax.dot_general(stacked[which_wave], table_rows, (((1,), (1,)), ((), ()))...  23.2 us
    unnamed x4, waiting for transfers between devices  17.3 us
    all_to_all x1, waiting for transfers between devices, body(): lax.all_to_all(masked, 'wave', split_axis=3, concat_axis=2, tiled=True)  15.7 us
    all_to_all x1, starting transfers between devices, body(): lax.all_to_all(masked, 'wave', split_axis=3, concat_axis=2, tiled=True)  8.3 us
    ppermute x15, waiting for transfers between devices, exchange_in_pairs(): lax.ppermute(sent, axis, [(i, i ^ hop) for i in range(devices)])  7.3 us
    unnamed x2, blocking collectives  5.99 us
  transfers between devices with their start and end apart: 19, of which 6 were waited for; matrix products, arithmetic and copies ran while one was open for 2% of the time, Pallas kernels for 0%

profile of v1, /device:TPU:0, one launch (start us, length us, event | category | flops | bytes accessed | tf_op | source)
XLA Modules:
  0.0 179.4 jit_solution(2642428775145617123)
XLA Ops:
  11.8 1.4 copy.61
  13.2 8.3 %all-to-all-start = ((bf16[3,14,80,64]{2,1,0,3:T(8,128)(2,1)}), bf16[3,14,80,64]{2,1,0,3:T(8,128)(2,1)S(1)}, u32[]{:S(2)}, u32[]{:S(2)}) async-start(bf16[3,14,80,64]{2,1,0,3:T(8,128)(2,1)} %copy.61), calls=%async_computation | async-start | bytes 1572864 | tf_op jit(solution)/shard_map/all_to_all | solution.py:133
  25.5 15.7 %all-to-all-done = bf16[3,14,80,64]{2,1,0,3:T(8,128)(2,1)S(1)} async-done(((bf16[3,14,80,64]{2,1,0,3:T(8,128)(2,1)}), bf16[3,14,80,64]{2,1,0,3:T(8,128)(2,1)S(1)}, u32[]{:S(2)}, u32[]{:S(2)}) %all-to-all-start) | async-done | bytes 430112 | tf_op jit(solution)/shard_map/all_to_all | solution.py:133
  43.2 19.2 %while.40 = (s32[]{:T(128)}, f32[84,1408]{0,1:T(8,128)S(1)}, s32[]{:T(128)}, bf16[1408,1280]{1,0:T(8,128)(2,1)}, bf16[2,84,1280]{2,1,0:T(8,128)(2,1)S(1)}, /*index=5*/s32[]{:T(128)}, s32[]{:T(128)}, s32[]{:T(128)}, s32[]{:T(128)}) while((s32[]{:T(128)}, f32[84,1408]{0,1:T(8,128)S(1)}, s32[]{:T(128)}, bf16[1408,1280]{1,0:T(8,128)(2,1)}, ...), condition=%wide.region_2.3_spmd, body=%wide.region_1.2_spmd.sunk | while | flops 13762566 | bytes 423059 | solution.py:73
  62.4 4.5 %while.41 = (s32[]{:T(128)}, f32[84,1408]{0,1:T(8,128)S(1)}, s32[]{:T(128)}, bf16[1408,1280]{1,0:T(8,128)(2,1)}, bf16[2,84,1280]{2,1,0:T(8,128)(2,1)S(1)}, /*index=5*/s32[]{:T(128)}, s32[]{:T(128)}, s32[]{:T(128)}, s32[]{:T(128)}) while((s32[]{:T(128)}, f32[84,1408]{0,1:T(8,128)S(1)}, s32[]{:T(128)}, bf16[1408,1280]{1,0:T(8,128)(2,1)}, ...), condition=%wide.region_4.5_spmd, body=%wide.region_3.4_spmd.sunk | while | flops 13762566 | bytes 423059 | solution.py:76
  68.6 3.0 %fusion = bf16[16,2816]{1,0:T(8,128)(2,1)S(1)} fusion(bf16[28,2816]{1,0:T(8,128)(2,1)S(1)} %convolution_convert_fusion.3), kind=kCustom, calls=%all-reduce-scatter | all-reduce-scatter fusion | flops 90113 | bytes 248320
  71.6 2.3 %collective-permute-start.15 = (bf16[2,2816]{1,0:T(2,128)(2,1)S(1)}, bf16[2,2816]{1,0:T(2,128)(2,1)S(1)}, u32[]{:S(2)}, u32[]{:S(2)}) collective-permute-start(bf16[2,2816]{1,0:T(2,128)(2,1)S(1)} %slice.54), channel_id=1, source_target_pairs={{0,1},{2,3},{4,5},{6,7},{8,9},{10,11},{12,13},{14,15},{16,17},{18,... | collective-permute-start | bytes 33800
  76.9 3.0 %fusion.1 = bf16[16,2816]{1,0:T(8,128)(2,1)S(1)} fusion(bf16[28,2816]{1,0:T(8,128)(2,1)S(1)} %convolution_convert_fusion.2), kind=kCustom, calls=%all-reduce-scatter.1 | all-reduce-scatter fusion | flops 90113 | bytes 248320
  80.0 2.3 %collective-permute-start.16 = (bf16[2,2816]{1,0:T(2,128)(2,1)S(1)}, bf16[2,2816]{1,0:T(2,128)(2,1)S(1)}, u32[]{:S(2)}, u32[]{:S(2)}) collective-permute-start(bf16[2,2816]{1,0:T(2,128)(2,1)S(1)} %slice.55), channel_id=1, source_target_pairs={{0,1},{2,3},{4,5},{6,7},{8,9},{10,11},{12,13},{14,15},{16,17},{18,... | collective-permute-start | bytes 33800
  86.7 16.6 %all-reduce.7.cloned.1.call-done = bf16[28,2,2816]{2,1,0:T(2,128)(2,1)} async-done(((bf16[28,2,2816]{2,1,0:T(2,128)(2,1)}), bf16[28,2,2816]{2,1,0:T(2,128)(2,1)}) %all-reduce.7.cloned.1.call-update) | async-done | bytes 315408
  105.4 4.9 %while.43 = (s32[]{:T(128)}, f32[84,1280]{1,0:T(8,128)S(1)}, s32[]{:T(128)}, bf16[84,1408]{1,0:T(8,128)(2,1)S(1)}, bf16[1408,1280]{1,0:T(8,128)(2,1)}, /*index=5*/s32[]{:T(128)}, s32[]{:T(128)}, s32[]{:T(128)}, s32[]{:T(128)}) while((s32[]{:T(128)}, f32[84,1280]{1,0:T(8,128)S(1)}, s32[]{:T(128)}, bf16[84,1408]{1,0:T(8,128)(2,1)S(1)}, ...), condition=%wide.region_11.12_spmd, body=%wide.region_10.11_spmd.sunk | while | flops 13870086 | bytes 1068179 | solution.py:99
  109.0 1.2 convolution_add_fusion.5
  110.4 20.9 %while.42 = (s32[]{:T(128)}, f32[84,1280]{1,0:T(8,128)S(1)}, s32[]{:T(128)}, bf16[84,1408]{1,0:T(8,128)(2,1)S(1)}, bf16[1408,1280]{1,0:T(8,128)(2,1)}, /*index=5*/s32[]{:T(128)}, s32[]{:T(128)}, s32[]{:T(128)}, s32[]{:T(128)}) while((s32[]{:T(128)}, f32[84,1280]{1,0:T(8,128)S(1)}, s32[]{:T(128)}, bf16[84,1408]{1,0:T(8,128)(2,1)S(1)}, ...), condition=%wide.region_9.10_spmd, body=%wide.region_8.9_spmd.sunk | while | flops 13870086 | bytes 1068179 | solution.py:98
  111.7 1.2 convolution_add_fusion.4
  114.1 1.2 convolution_add_fusion.4
  116.5 1.2 convolution_add_fusion.4
  119.0 1.2 convolution_add_fusion.4
  121.4 1.2 convolution_add_fusion.4
  132.9 1.7 constant_dynamic-slice_fusion
  134.5 1.8 %collective-permute-start = (bf16[3,14,80,4]{2,3,1,0:T(4,128)(2,1)S(1)}, bf16[3,14,80,4]{2,3,1,0:T(4,128)(2,1)S(1)}, u32[]{:S(2)}, u32[]{:S(2)}) collective-permute-start(bf16[3,14,80,4]{2,3,1,0:T(4,128)(2,1)S(1)} %bitcast.196), channel_id=1, source_target_pairs={{0,2},{2,0},{4,6},{6,4},{8,10},{10,8},{12,14},{14,12},{16,18},{18,... | collective-permute-start | bytes 80648 | tf_op jit(solution)/shard_map/ppermute | solution.py:29
  136.4 1.5 collective-permute-start.1
  138.3 1.8 %collective-permute-start.3 = (bf16[3,14,80,4]{2,3,1,0:T(4,128)(2,1)S(1)}, bf16[3,14,80,4]{2,3,1,0:T(4,128)(2,1)S(1)}, u32[]{:S(2)}, u32[]{:S(2)}) collective-permute-start(bf16[3,14,80,4]{2,3,1,0:T(4,128)(2,1)S(1)} %bitcast.193), channel_id=1, source_target_pairs={{0,8},{2,10},{4,12},{6,14},{8,0},{10,2},{12,4},{14,6},{16,24},{18,... | collective-permute-start | bytes 80648 | tf_op jit(solution)/shard_map/ppermute | solution.py:29
  140.2 1.5 collective-permute-start.4
  142.0 2.5 %collective-permute-start.5 = (bf16[3,14,80,4]{2,3,1,0:T(4,128)(2,1)S(1)}, bf16[3,14,80,4]{2,3,1,0:T(4,128)(2,1)S(1)}, u32[]{:S(2)}, u32[]{:S(2)}) collective-permute-start(bf16[3,14,80,4]{2,3,1,0:T(4,128)(2,1)S(1)} %bitcast.191), channel_id=1, source_target_pairs={{0,12},{2,14},{4,8},{6,10},{8,4},{10,6},{12,0},{14,2},{16,28},{18,... | collective-permute-start | bytes 80648 | tf_op jit(solution)/shard_map/ppermute | solution.py:29
  144.8 2.8 %collective-permute-start.7 = (bf16[3,14,80,4]{2,3,1,0:T(4,128)(2,1)S(1)}, bf16[3,14,80,4]{2,3,1,0:T(4,128)(2,1)S(1)}, u32[]{:S(2)}, u32[]{:S(2)}) collective-permute-start(bf16[3,14,80,4]{2,3,1,0:T(4,128)(2,1)S(1)} %bitcast.189), channel_id=1, source_target_pairs={{0,16},{2,18},{4,20},{6,22},{8,24},{10,26},{12,28},{14,30},{16,0},... | collective-permute-start | bytes 80648 | tf_op jit(solution)/shard_map/ppermute | solution.py:29
  147.6 1.5 collective-permute-start.8
  149.1 3.4 %collective-permute-start.9 = (bf16[3,14,80,4]{2,3,1,0:T(4,128)(2,1)S(1)}, bf16[3,14,80,4]{2,3,1,0:T(4,128)(2,1)S(1)}, u32[]{:S(2)}, u32[]{:S(2)}) collective-permute-start(bf16[3,14,80,4]{2,3,1,0:T(4,128)(2,1)S(1)} %bitcast.187), channel_id=1, source_target_pairs={{0,20},{2,22},{4,16},{6,18},{8,28},{10,30},{12,24},{14,26},{16,4},... | collective-permute-start | bytes 80648 | tf_op jit(solution)/shard_map/ppermute | solution.py:29
  152.8 3.7 %collective-permute-start.11 = (bf16[3,14,80,4]{2,3,1,0:T(4,128)(2,1)S(1)}, bf16[3,14,80,4]{2,3,1,0:T(4,128)(2,1)S(1)}, u32[]{:S(2)}, u32[]{:S(2)}) collective-permute-start(bf16[3,14,80,4]{2,3,1,0:T(4,128)(2,1)S(1)} %bitcast.185), channel_id=1, source_target_pairs={{0,24},{2,26},{4,28},{6,30},{8,16},{10,18},{12,20},{14,22},{16,8},... | collective-permute-start | bytes 80648 | tf_op jit(solution)/shard_map/ppermute | solution.py:29
  156.6 1.5 collective-permute-start.12
  158.1 4.3 %collective-permute-start.13 = (bf16[3,14,80,4]{2,3,1,0:T(4,128)(2,1)S(1)}, bf16[3,14,80,4]{2,3,1,0:T(4,128)(2,1)S(1)}, u32[]{:S(2)}, u32[]{:S(2)}) collective-permute-start(bf16[3,14,80,4]{2,3,1,0:T(4,128)(2,1)S(1)} %bitcast.183), channel_id=1, source_target_pairs={{0,28},{2,30},{4,24},{6,26},{8,20},{10,22},{12,16},{14,18},{16,12}... | collective-permute-start | bytes 80648 | tf_op jit(solution)/shard_map/ppermute | solution.py:29
  163.4 2.0 %collective-permute-done.13 = bf16[3,14,80,4]{2,3,1,0:T(4,128)(2,1)S(1)} collective-permute-done((bf16[3,14,80,4]{2,3,1,0:T(4,128)(2,1)S(1)}, bf16[3,14,80,4]{2,3,1,0:T(4,128)(2,1)S(1)}, u32[]{:S(2)}, u32[]{:S(2)}) %collective-permute-start.13) | collective-permute-done | bytes 26912 | tf_op jit(solution)/shard_map/ppermute | solution.py:29
  165.4 4.7 %collective-permute-done.14 = bf16[3,14,80,4]{2,3,1,0:T(4,128)(2,1)S(1)} collective-permute-done((bf16[3,14,80,4]{2,3,1,0:T(4,128)(2,1)S(1)}, bf16[3,14,80,4]{2,3,1,0:T(4,128)(2,1)S(1)}, u32[]{:S(2)}, u32[]{:S(2)}) %collective-permute-start.14) | collective-permute-done | bytes 26912 | tf_op jit(solution)/shard_map/ppermute | solution.py:29
  (168 shorter events, 64.3 us)
Async XLA Ops:
  7.2 60.9 %copy-start = (f32[28,28]{1,0:T(8,128)S(1)}, f32[28,28]{1,0:T(8,128)}, u32[]{:S(2)}) copy-start(f32[28,28]{1,0:T(8,128)} %param.22) | copy-start | bytes 9412
  7.2 14.3 %copy-start.4 = (s32[16]{0:T(128)S(1)}, s32[16]{0:T(128)}, u32[]{:S(2)}) copy-start(s32[16]{0:T(128)} %param.27) | copy-start | bytes 196
  7.2 17.6 %copy-start.1 = (bf16[3,14,1,2816]{3,1,2,0:T(8,128)(2,1)S(1)}, bf16[3,14,1,2816]{3,1,2,0:T(8,128)(2,1)}, u32[]{:S(2)}) copy-start(bf16[3,14,1,2816]{3,1,2,0:T(8,128)(2,1)} %param.20) | copy-start | bytes 709636
  13.2 28.1 %all-to-all-start = ((bf16[3,14,80,64]{2,1,0,3:T(8,128)(2,1)}), bf16[3,14,80,64]{2,1,0,3:T(8,128)(2,1)S(1)}, u32[]{:S(2)}, u32[]{:S(2)}) async-start(bf16[3,14,80,64]{2,1,0,3:T(8,128)(2,1)} %copy.61), calls=%async_computation | async-start | bytes 1572864 | tf_op jit(solution)/shard_map/all_to_all | solution.py:133
  21.5 81.8 %all-reduce.7.cloned.1.call-start = ((), (), s32[]{:S(2)}) async-start(), calls=%async_computation.1 | async-start | bytes 630784
  67.0 7.6 %copy-start.3 = (u32[32]{0:T(128)S(1)}, u32[32]{0:T(128)}, u32[]{:S(2)}) copy-start(u32[32]{0:T(128)} %constant.144) | copy-start | bytes 388
  67.3 9.2 %copy-start.2 = (f32[28,28]{1,0:T(8,128)S(1)}, f32[28,28]{1,0:T(8,128)}, u32[]{:S(2)}) copy-start(f32[28,28]{1,0:T(8,128)} %param.23) | copy-start | bytes 9412
  67.3 15.0 %copy-start.7 = (f32[28]{0:T(128)S(1)}, f32[28]{0:T(128)}, u32[]{:S(2)}) copy-start(f32[28]{0:T(128)} %param.26) | copy-start | bytes 340
  67.3 16.1 %copy-start.5 = (f32[28,28]{1,0:T(8,128)S(1)}, f32[28,28]{1,0:T(8,128)}, u32[]{:S(2)}) copy-start(f32[28,28]{1,0:T(8,128)} %param.25) | copy-start | bytes 9412
  67.7 16.1 %copy-start.6 = (f32[28,28]{1,0:T(8,128)S(1)}, f32[28,28]{1,0:T(8,128)}, u32[]{:S(2)}) copy-start(f32[28,28]{1,0:T(8,128)} %param.24) | copy-start | bytes 9412
  71.6 4.5 %collective-permute-start.15 = (bf16[2,2816]{1,0:T(2,128)(2,1)S(1)}, bf16[2,2816]{1,0:T(2,128)(2,1)S(1)}, u32[]{:S(2)}, u32[]{:S(2)}) collective-permute-start(bf16[2,2816]{1,0:T(2,128)(2,1)S(1)} %slice.54), channel_id=1, source_target_pairs={{0,1},{2,3},{4,5},{6,7},{8,9},{10,11},{12,13},{14,15},{16,17},{18,... | collective-permute-start | bytes 33800
  80.0 3.1 %collective-permute-start.16 = (bf16[2,2816]{1,0:T(2,128)(2,1)S(1)}, bf16[2,2816]{1,0:T(2,128)(2,1)S(1)}, u32[]{:S(2)}, u32[]{:S(2)}) collective-permute-start(bf16[2,2816]{1,0:T(2,128)(2,1)S(1)} %slice.55), channel_id=1, source_target_pairs={{0,1},{2,3},{4,5},{6,7},{8,9},{10,11},{12,13},{14,15},{16,17},{18,... | collective-permute-start | bytes 33800
  134.5 7.4 %collective-permute-start = (bf16[3,14,80,4]{2,3,1,0:T(4,128)(2,1)S(1)}, bf16[3,14,80,4]{2,3,1,0:T(4,128)(2,1)S(1)}, u32[]{:S(2)}, u32[]{:S(2)}) collective-permute-start(bf16[3,14,80,4]{2,3,1,0:T(4,128)(2,1)S(1)} %bitcast.196), channel_id=1, source_target_pairs={{0,2},{2,0},{4,6},{6,4},{8,10},{10,8},{12,14},{14,12},{16,18},{18,... | collective-permute-start | bytes 80648 | tf_op jit(solution)/shard_map/ppermute | solution.py:29
  136.4 8.0 %collective-permute-start.1 = (bf16[3,14,80,4]{2,3,1,0:T(4,128)(2,1)S(1)}, bf16[3,14,80,4]{2,3,1,0:T(4,128)(2,1)S(1)}, u32[]{:S(2)}, u32[]{:S(2)}) collective-permute-start(bf16[3,14,80,4]{2,3,1,0:T(4,128)(2,1)S(1)} %bitcast.195), channel_id=1, source_target_pairs={{0,4},{2,6},{4,0},{6,2},{8,12},{10,14},{12,8},{14,10},{16,20},{18,... | collective-permute-start | bytes 80648 | tf_op jit(solution)/shard_map/ppermute | solution.py:29
  138.0 6.8 %collective-permute-start.2 = (bf16[3,14,80,4]{2,3,1,0:T(4,128)(2,1)S(1)}, bf16[3,14,80,4]{2,3,1,0:T(4,128)(2,1)S(1)}, u32[]{:S(2)}, u32[]{:S(2)}) collective-permute-start(bf16[3,14,80,4]{2,3,1,0:T(4,128)(2,1)S(1)} %bitcast.194), channel_id=1, source_target_pairs={{0,6},{2,4},{4,2},{6,0},{8,14},{10,12},{12,10},{14,8},{16,22},{18,... | collective-permute-start | bytes 80648 | tf_op jit(solution)/shard_map/ppermute | solution.py:29
  138.3 9.3 %collective-permute-start.3 = (bf16[3,14,80,4]{2,3,1,0:T(4,128)(2,1)S(1)}, bf16[3,14,80,4]{2,3,1,0:T(4,128)(2,1)S(1)}, u32[]{:S(2)}, u32[]{:S(2)}) collective-permute-start(bf16[3,14,80,4]{2,3,1,0:T(4,128)(2,1)S(1)} %bitcast.193), channel_id=1, source_target_pairs={{0,8},{2,10},{4,12},{6,14},{8,0},{10,2},{12,4},{14,6},{16,24},{18,... | collective-permute-start | bytes 80648 | tf_op jit(solution)/shard_map/ppermute | solution.py:29
  140.2 8.9 %collective-permute-start.4 = (bf16[3,14,80,4]{2,3,1,0:T(4,128)(2,1)S(1)}, bf16[3,14,80,4]{2,3,1,0:T(4,128)(2,1)S(1)}, u32[]{:S(2)}, u32[]{:S(2)}) collective-permute-start(bf16[3,14,80,4]{2,3,1,0:T(4,128)(2,1)S(1)} %bitcast.192), channel_id=1, source_target_pairs={{0,10},{2,8},{4,14},{6,12},{8,2},{10,0},{12,6},{14,4},{16,26},{18,... | collective-permute-start | bytes 80648 | tf_op jit(solution)/shard_map/ppermute | solution.py:29
  142.0 10.6 %collective-permute-start.5 = (bf16[3,14,80,4]{2,3,1,0:T(4,128)(2,1)S(1)}, bf16[3,14,80,4]{2,3,1,0:T(4,128)(2,1)S(1)}, u32[]{:S(2)}, u32[]{:S(2)}) collective-permute-start(bf16[3,14,80,4]{2,3,1,0:T(4,128)(2,1)S(1)} %bitcast.191), channel_id=1, source_target_pairs={{0,12},{2,14},{4,8},{6,10},{8,4},{10,6},{12,0},{14,2},{16,28},{18,... | collective-permute-start | bytes 80648 | tf_op jit(solution)/shard_map/ppermute | solution.py:29
  144.4 8.4 %collective-permute-start.6 = (bf16[3,14,80,4]{2,3,1,0:T(4,128)(2,1)S(1)}, bf16[3,14,80,4]{2,3,1,0:T(4,128)(2,1)S(1)}, u32[]{:S(2)}, u32[]{:S(2)}) collective-permute-start(bf16[3,14,80,4]{2,3,1,0:T(4,128)(2,1)S(1)} %bitcast.190), channel_id=1, source_target_pairs={{0,14},{2,12},{4,10},{6,8},{8,6},{10,4},{12,2},{14,0},{16,30},{18,... | collective-permute-start | bytes 80648 | tf_op jit(solution)/shard_map/ppermute | solution.py:29
  144.8 11.8 %collective-permute-start.7 = (bf16[3,14,80,4]{2,3,1,0:T(4,128)(2,1)S(1)}, bf16[3,14,80,4]{2,3,1,0:T(4,128)(2,1)S(1)}, u32[]{:S(2)}, u32[]{:S(2)}) collective-permute-start(bf16[3,14,80,4]{2,3,1,0:T(4,128)(2,1)S(1)} %bitcast.189), channel_id=1, source_target_pairs={{0,16},{2,18},{4,20},{6,22},{8,24},{10,26},{12,28},{14,30},{16,0},... | collective-permute-start | bytes 80648 | tf_op jit(solution)/shard_map/ppermute | solution.py:29
  147.6 10.5 %collective-permute-start.8 = (bf16[3,14,80,4]{2,3,1,0:T(4,128)(2,1)S(1)}, bf16[3,14,80,4]{2,3,1,0:T(4,128)(2,1)S(1)}, u32[]{:S(2)}, u32[]{:S(2)}) collective-permute-start(bf16[3,14,80,4]{2,3,1,0:T(4,128)(2,1)S(1)} %bitcast.188), channel_id=1, source_target_pairs={{0,18},{2,16},{4,22},{6,20},{8,26},{10,24},{12,30},{14,28},{16,2},... | collective-permute-start | bytes 80648 | tf_op jit(solution)/shard_map/ppermute | solution.py:29
  149.1 13.3 %collective-permute-start.9 = (bf16[3,14,80,4]{2,3,1,0:T(4,128)(2,1)S(1)}, bf16[3,14,80,4]{2,3,1,0:T(4,128)(2,1)S(1)}, u32[]{:S(2)}, u32[]{:S(2)}) collective-permute-start(bf16[3,14,80,4]{2,3,1,0:T(4,128)(2,1)S(1)} %bitcast.187), channel_id=1, source_target_pairs={{0,20},{2,22},{4,16},{6,18},{8,28},{10,30},{12,24},{14,26},{16,4},... | collective-permute-start | bytes 80648 | tf_op jit(solution)/shard_map/ppermute | solution.py:29
  152.5 10.2 %collective-permute-start.10 = (bf16[3,14,80,4]{2,3,1,0:T(4,128)(2,1)S(1)}, bf16[3,14,80,4]{2,3,1,0:T(4,128)(2,1)S(1)}, u32[]{:S(2)}, u32[]{:S(2)}) collective-permute-start(bf16[3,14,80,4]{2,3,1,0:T(4,128)(2,1)S(1)} %bitcast.186), channel_id=1, source_target_pairs={{0,22},{2,20},{4,18},{6,16},{8,30},{10,28},{12,26},{14,24},{16,6},... | collective-permute-start | bytes 80648 | tf_op jit(solution)/shard_map/ppermute | solution.py:29
  152.8 9.9 %collective-permute-start.11 = (bf16[3,14,80,4]{2,3,1,0:T(4,128)(2,1)S(1)}, bf16[3,14,80,4]{2,3,1,0:T(4,128)(2,1)S(1)}, u32[]{:S(2)}, u32[]{:S(2)}) collective-permute-start(bf16[3,14,80,4]{2,3,1,0:T(4,128)(2,1)S(1)} %bitcast.185), channel_id=1, source_target_pairs={{0,24},{2,26},{4,28},{6,30},{8,16},{10,18},{12,20},{14,22},{16,8},... | collective-permute-start | bytes 80648 | tf_op jit(solution)/shard_map/ppermute | solution.py:29
  156.6 6.8 %collective-permute-start.12 = (bf16[3,14,80,4]{2,3,1,0:T(4,128)(2,1)S(1)}, bf16[3,14,80,4]{2,3,1,0:T(4,128)(2,1)S(1)}, u32[]{:S(2)}, u32[]{:S(2)}) collective-permute-start(bf16[3,14,80,4]{2,3,1,0:T(4,128)(2,1)S(1)} %bitcast.184), channel_id=1, source_target_pairs={{0,26},{2,24},{4,30},{6,28},{8,18},{10,16},{12,22},{14,20},{16,10}... | collective-permute-start | bytes 80648 | tf_op jit(solution)/shard_map/ppermute | solution.py:29
  158.1 7.3 %collective-permute-start.13 = (bf16[3,14,80,4]{2,3,1,0:T(4,128)(2,1)S(1)}, bf16[3,14,80,4]{2,3,1,0:T(4,128)(2,1)S(1)}, u32[]{:S(2)}, u32[]{:S(2)}) collective-permute-start(bf16[3,14,80,4]{2,3,1,0:T(4,128)(2,1)S(1)} %bitcast.183), channel_id=1, source_target_pairs={{0,28},{2,30},{4,24},{6,26},{8,20},{10,22},{12,16},{14,18},{16,12}... | collective-permute-start | bytes 80648 | tf_op jit(solution)/shard_map/ppermute | solution.py:29
  162.4 7.7 %collective-permute-start.14 = (bf16[3,14,80,4]{2,3,1,0:T(4,128)(2,1)S(1)}, bf16[3,14,80,4]{2,3,1,0:T(4,128)(2,1)S(1)}, u32[]{:S(2)}, u32[]{:S(2)}) collective-permute-start(bf16[3,14,80,4]{2,3,1,0:T(4,128)(2,1)S(1)} %bitcast.182), channel_id=1, source_target_pairs={{0,30},{2,28},{4,26},{6,24},{8,22},{10,20},{12,18},{14,16},{16,14}... | collective-permute-start | bytes 80648 | tf_op jit(solution)/shard_map/ppermute | solution.py:29
Sparse Core Ops, SparseCore 0:
  85.6 17.6 all-reduce.6
